TPU v7x, 256 devices: a whole 4x4x8 slice. The times are simulated.
256 devices in a mesh: east: 8 (over z_hi, core), north: 32 (over y, z_lo, x).
Axes of the slice: x: 4, y: 4, z: 8 (z_hi: 4, z_lo: 2; z = z_hi * 2 + z_lo), core: 2. Of those that a mesh axis runs over, the one named last changes fastest.
Arguments:
- adjoint_start: float32 [5, 128, 1024, 256], P(None, 'east', 'north'), may hold values from -3 to 3
- adjoint_source: float32 [5, 128, 1024, 256], P(None, 'east', 'north'), may hold values from -6 to 6
- base_flow: float32 [3, 128, 1024, 256], P(None, 'east', 'north'), may hold values from -3 to 3
- eddy_visc: float32 [128, 1024, 256], P('east', 'north'), may hold values from 0.1 to 3
- rotor_count: int32 [8, 32], P('east', 'north'), may hold values from 128 to 1024, as said below
- rotor_cell: int32 [8, 32, 1024], P('east', 'north'), may hold values from 0 to 131071
- rotor_turbine: int32 [8, 32, 1024], P('east', 'north'), may hold values from 0 to 383
- rotor_sector: int32 [8, 32, 1024], P('east', 'north'), may hold values from 0 to 7
- rotor_weight: float32 [8, 32, 1024], P('east', 'north'), may hold values from 0.25 to 1
Outputs:
- adjoint_final: float32 [5, 128, 1024, 256], P(None, 'east', 'north')
- thrust_grad: float32 [4, 8, 384], P(None, None, 'north')
Inputs may be any that keep to these rules, and one draw needn't show every extreme that they name: `rotor_count`: an eighth of the tiles (at least one), drawn from the seed, hold 1024 live entries; the others hold 128 to 256.
All inputs are finite; a program needn't handle non-finite values.
Results may differ from a plain program's by a relative error of at most 0.0001.
Values sent between devices are 32-bit elements; how exact they have to be, the bound alone decides.
A program may use at most 192 MiB of HBM per device.

v0:
```python
import jax
import jax.numpy as jnp
from jax import lax
from jax.sharding import PartitionSpec as P

SECT = 8
TURB_DEV = 12


def extended(shard, sides, width):
    for axis, dim in sides:
        size, length = (lax.axis_size(axis), shard.shape[dim])
        up = [(i, (i + 1) % size) for i in range(size - 1)]
        down = [(j, i) for i, j in up]
        last = lax.slice_in_dim(shard, length - width, length, axis=dim)
        leading = lax.slice_in_dim(shard, 0, width, axis=dim)
        before = lax.ppermute(last, axis, up)
        after = lax.ppermute(leading, axis, down)
        shard = jnp.concatenate([before, shard, after], axis=dim)
    return shard


def spread(field):
    return jnp.pad(field, ((0, 0), (0, 0), (0, 0), (1, 1)))


def beside_all(padded):
    total = padded[:, 2:, 1:-1, 1:-1] + padded[:, :-2, 1:-1, 1:-1]
    total = total + padded[:, 1:-1, 2:, 1:-1] + padded[:, 1:-1, :-2, 1:-1]
    return total + padded[:, 1:-1, 1:-1, 2:] + padded[:, 1:-1, 1:-1, :-2]


def slopes(padded):
    return [
        padded[:, 2:, 1:-1, 1:-1] - padded[:, :-2, 1:-1, 1:-1],
        padded[:, 1:-1, 2:, 1:-1] - padded[:, 1:-1, :-2, 1:-1],
        padded[:, 1:-1, 1:-1, 2:] - padded[:, 1:-1, 1:-1, :-2],
    ]


def relax(state_pad, base_pad, source):
    full = spread(state_pad)
    base_full = spread(base_pad)
    centre = full[:, 1:-1, 1:-1, 1:-1]
    base_centre = base_full[:, 1:-1, 1:-1, 1:-1]
    neighbours = beside_all(full)
    diffs = slopes(full)
    velocity_base = base_centre[:3]
    viscous = 1.0 + base_centre[3]
    convect = (
        velocity_base[0] * diffs[0][:3]
        + velocity_base[1] * diffs[1][:3]
        + velocity_base[2] * diffs[2][:3]
    )
    pressure_grad = jnp.stack([diffs[0][3], diffs[1][3], diffs[2][3]])
    velocity = (source[:3] + viscous * neighbours[:3] + 0.5 * convect - 0.5 * pressure_grad) / (
        6.0 * viscous + 1.0
    )
    diverge = diffs[0][0] + diffs[1][1] + diffs[2][2]
    pressure = (source[3] + neighbours[3] - 0.5 * diverge) / 7.0
    curvature = beside_all(base_full[:3]) - 6.0 * velocity_base
    eddy_new = (
        source[4] + viscous * neighbours[4] + 0.25 * jnp.sum(centre[:3] * curvature, axis=0)
    ) / (6.0 * viscous + 2.0)
    return jnp.concatenate([velocity, pressure[None], eddy_new[None]], axis=0)


def shards(
    adjoint_start,
    adjoint_source,
    base_flow,
    eddy_visc,
    rotor_count,
    rotor_cell,
    rotor_turbine,
    rotor_sector,
    rotor_weight,
):
    base_four = jnp.concatenate([base_flow, eddy_visc[None]], axis=0)
    base_pad = extended(base_four, (("east", 1), ("north", 2)), 1)
    state = adjoint_start
    for sweep in range(2):
        state_pad = extended(state, (("east", 1), ("north", 2)), 1)
        state = relax(state_pad, base_pad, adjoint_source)
    cells = rotor_cell.reshape(-1)
    flat_state = state.reshape(5, -1)
    values = flat_state[:, cells]
    chosen = jnp.stack([values[0], values[1], values[2], values[4]])
    upstream = base_flow[0].reshape(-1)[cells]
    slot_count = cells.shape[0]
    live = jnp.arange(slot_count, dtype=jnp.int32) < rotor_count.reshape(-1)[0]
    factor = jnp.where(live, rotor_weight.reshape(-1) * upstream * jnp.abs(upstream), 0.0)
    terms = chosen * factor[None]
    sector_hot = (
        rotor_sector.reshape(-1)[None, :] == jnp.arange(SECT, dtype=jnp.int32)[:, None]
    ).astype(jnp.float32)
    combined = (terms[:, None, :] * sector_hot[None]).reshape(4 * SECT, slot_count)
    turbine_total_count = TURB_DEV * lax.axis_size("north")
    turbine_hot = (
        rotor_turbine.reshape(-1)[:, None]
        == jnp.arange(turbine_total_count, dtype=jnp.int32)[None, :]
    ).astype(jnp.float32)
    partial_grad = jnp.dot(
        combined, turbine_hot, precision=lax.Precision.HIGHEST, preferred_element_type=jnp.float32
    )
    summed = lax.psum(partial_grad, ("east", "north"))
    owned = lax.dynamic_slice_in_dim(summed, lax.axis_index("north") * TURB_DEV, TURB_DEV, 1)
    return (state, owned.reshape(4, SECT, TURB_DEV))


def solution(mesh):
    placed = (
        P(None, "east", "north", None),
        P(None, "east", "north", None),
        P(None, "east", "north", None),
        P("east", "north", None),
        P("east", "north"),
        P("east", "north", None),
        P("east", "north", None),
        P("east", "north", None),
        P("east", "north", None),
    )
    return jax.shard_map(
        shards,
        mesh=mesh,
        in_specs=placed,
        out_specs=(P(None, "east", "north", None), P(None, None, "north")),
        check_vma=False,
    )
```

profile of v0, /device:TPU:1, one launch (start us, length us, event | category | flops | bytes accessed | tf_op | source)
XLA Modules:
  0.0 241.2 jit_solution(15971372391863261522)
XLA Ops:
  0.6 1.9 pad_maximum_fusion.37
  2.5 6.3 %collective-permute-start.5 = (f32[4,1,32,256]{3,2,1,0:T(8,128)}, f32[4,1,32,256]{3,2,1,0:T(8,128)}, u32[]{:S(2)}, u32[]{:S(2)}) collective-permute-start(f32[4,1,32,256]{3,2,1,0:T(8,128)} %get-tuple-element.27), channel_id=1, source_target_pairs={{0,32},{32,64},{64,96},{96,128},{128,160},{160,192},{192,224},{1,3... | collective-permute-start | bytes 393224 | tf_op jit(solution)/shard_map/ppermute | solution.py:17
  8.8 1.9 collective-permute-start.4
  10.7 1.7 fusion.45
  12.5 1.9 collective-permute-start
  14.4 0.0 copy-start.14
  14.4 0.0 copy-start.12
  14.4 4.5 %collective-permute-start.1 = (f32[5,1,32,256]{3,2,1,0:T(8,128)}, f32[5,1,32,256]{3,2,1,0:T(8,128)S(1)}, u32[]{:S(2)}, u32[]{:S(2)}) collective-permute-start(f32[5,1,32,256]{3,2,1,0:T(8,128)} %get-tuple-element.24), channel_id=1, source_target_pairs={{0,32},{32,64},{64,96},{96,128},{128,160},{160,192},{192,224},{1,3... | collective-permute-start | bytes 491528 | tf_op jit(solution)/shard_map/ppermute | solution.py:17
  19.0 0.9 broadcast_add_fusion
  19.9 1.5 fusion.46
  21.4 0.6 fusion.42
  22.7 1.3 copy.25
  24.0 6.2 %gather_fusion.1 = f32[1024]{0:T(1024)S(1)} fusion(f32[131072]{0:T(1024)S(1)} %bitcast.42, s32[1024]{0:T(1024)S(1)} %broadcast_clamp_fusion), kind=kCustom, calls=%fused_computation.1 | custom fusion | bytes 12288 | tf_op jit(solution)/shard_map/gather | solution.py:89
  30.1 0.0 copy-start.2
  30.2 0.0 collective-permute-done.5
  30.2 1.1 pad_maximum_fusion.44
  31.2 3.1 %collective-permute-start.7 = (f32[4,18,1,256]{3,2,1,0:T(1,128)S(1)}, f32[4,18,1,256]{3,2,1,0:T(1,128)S(1)}, u32[]{:S(2)}, u32[]{:S(2)}) collective-permute-start(f32[4,18,1,256]{3,2,1,0:T(1,128)S(1)} %get-tuple-element.25), channel_id=1, source_target_pairs={{0,1},{1,2},{2,3},{3,4},{4,5},{5,6},{6,7},{7,8},{8,9},{9,10},{10,1... | collective-permute-start | bytes 221192 | tf_op jit(solution)/shard_map/ppermute | solution.py:17
  34.4 1.3 collective-permute-start.6
  35.7 0.0 collective-permute-done.1
  35.7 0.6 fusion.2
  36.3 0.0 copy-start.3
  36.4 0.1 fusion.44
  36.5 4.0 %collective-permute-start.3 = (f32[5,18,1,256]{3,2,1,0:T(1,128)S(1)}, f32[5,18,1,256]{3,2,1,0:T(1,128)S(1)}, u32[]{:S(2)}, u32[]{:S(2)}) collective-permute-start(f32[5,18,1,256]{3,2,1,0:T(1,128)S(1)} %get-tuple-element.14), channel_id=1, source_target_pairs={{0,1},{1,2},{2,3},{3,4},{4,5},{5,6},{6,7},{7,8},{8,9},{9,10},{10,1... | collective-permute-start | bytes 276488 | tf_op jit(solution)/shard_map/ppermute | solution.py:17
  40.5 1.3 collective-permute-start.2
  41.8 0.8 slice.359
  42.6 0.0 collective-permute-done.7
  42.6 0.0 collective-permute-done.6
  42.6 5.5 %select_maximum_fusion.8 = f32[4,18,34,258]{3,2,1,0:T(8,128)S(1)} fusion(f32[4,18,1,256]{3,2,1,0:T(1,128)S(1)} %collective-permute-done.6, f32[4,18,1,256]{3,2,1,0:T(1,128)S(1)} %collective-permute-done.7, f32[4,1,32,256]{3,2,1,0:T(8,128)} %collective-permute-done.4, f32[4,1,32,256]{3,2,1,0:T(8,128)} %collective-permute-done.5, ...), kind=kLoop, calls=%fused_computation.15 | loop fusion | flops 8842176 | bytes 5033088 | tf_op jit(solution)/shard_map/concatenate | solution.py:19
  48.2 0.0 collective-permute-done.3
  48.2 0.0 collective-permute-done.2
  48.2 3.0 %select_maximum_fusion.6 = f32[5,18,34,258]{3,2,1,0:T(8,128)S(1)} fusion(f32[5,18,1,256]{3,2,1,0:T(1,128)S(1)} %collective-permute-done.2, f32[5,18,32,256]{3,2,1,0:T(8,128)S(1)} %constant_dynamic-update-slice_fusion, f32[5,18,1,256]{3,2,1,0:T(1,128)S(1)} %collective-permute-done.3), kind=kLoop, calls=%fused_computation.12 | loop fusion | flops 6315840 | bytes 6291360 | tf_op jit(solution)/shard_map/concatenate | solution.py:19
  51.3 3.6 %slice_subtract_fusion.1 = (f32[5,16,32,256]{3,2,1,0:T(8,128)S(1)}, f32[5,16,32,256]{3,2,1,0:T(8,128)S(1)}, f32[5,16,32,256]{3,2,1,0:T(8,128)S(1)}) fusion(f32[5,18,34,258]{3,2,1,0:T(8,128)S(1)} %select_maximum_fusion.6, f32[5,18,32,256]{3,2,1,0:T(8,128)S(1)} %constant_dynamic-update-slice_fusion, f32[5,18,1,256]{3,2,1,0:T(1,128)S(1)} %collective-permute-done.3, ...), kind=kLoop, calls=%fused_computation.46 | loop fusion | flops 7208960 | bytes 19189760 | tf_op jit(solution)/shard_map/sub | solution.py:37
  55.0 5.9 %multiply_reduce_fusion = (f32[16,32,256]{2,1,0:T(8,128)}, f32[16,32,256]{2,1,0:T(8,128)}, f32[3,16,32,256]{3,2,1,0:T(8,128)S(1)}) fusion(f32[5,16,32,256]{3,2,1,0:T(8,128)S(1)} %copy-done.2, f32[16,32,256]{2,1,0:T(8,128)S(1)} %copy-done.5, f32[1,16,32,256]{3,2,1,0:T(8,128)S(1)} %slice.361, f32[1,16,32,256]{3,2,1,0:T(8,128)S(1)} %slice.360, ...), kind=kLoop, calls=%fused_computation.92 | loop fusion | flops 14286848 | bytes 21905408 | tf_op jit(solution)/shard_map/reduce_sum | solution.py:63
  60.9 2.0 fusion.37
  63.0 0.0 copy-start.13
  63.0 4.7 %collective-permute-start.9 = (f32[5,1,32,256]{3,2,1,0:T(8,128)S(1)}, f32[5,1,32,256]{3,2,1,0:T(8,128)S(1)}, u32[]{:S(2)}, u32[]{:S(2)}) collective-permute-start(f32[5,1,32,256]{3,2,1,0:T(8,128)S(1)} %get-tuple-element.19), channel_id=1, source_target_pairs={{0,32},{32,64},{64,96},{96,128},{128,160},{160,192},{192,224},{1,3... | collective-permute-start | bytes 491528 | tf_op jit(solution)/shard_map/ppermute | solution.py:17
  67.7 1.9 collective-permute-start.8
  69.7 0.3 collective-permute-done.9
  70.0 5.7 %collective-permute-done.8 = f32[5,1,32,256]{3,2,1,0:T(8,128)S(1)} collective-permute-done((f32[5,1,32,256]{3,2,1,0:T(8,128)S(1)}, f32[5,1,32,256]{3,2,1,0:T(8,128)S(1)}, u32[]{:S(2)}, u32[]{:S(2)}) %collective-permute-start.8) | collective-permute-done | bytes 163872 | tf_op jit(solution)/shard_map/ppermute | solution.py:18
  75.6 0.1 pad_maximum_fusion.39
  75.8 5.7 %collective-permute-start.11 = (f32[5,18,1,256]{3,2,1,0:T(1,128)S(1)}, f32[5,18,1,256]{3,2,1,0:T(1,128)S(1)}, u32[]{:S(2)}, u32[]{:S(2)}) collective-permute-start(f32[5,18,1,256]{3,2,1,0:T(1,128)S(1)} %get-tuple-element.12), channel_id=1, source_target_pairs={{0,1},{1,2},{2,3},{3,4},{4,5},{5,6},{6,7},{7,8},{8,9},{9,10},{10,1... | collective-permute-start | bytes 276488 | tf_op jit(solution)/shard_map/ppermute | solution.py:17
  81.5 1.3 collective-permute-start.10
  82.8 0.4 fusion.23
  83.3 3.5 %collective-permute-done.10 = f32[5,18,1,256]{3,2,1,0:T(1,128)S(1)} collective-permute-done((f32[5,18,1,256]{3,2,1,0:T(1,128)S(1)}, f32[5,18,1,256]{3,2,1,0:T(1,128)S(1)}, u32[]{:S(2)}, u32[]{:S(2)}) %collective-permute-start.10) | collective-permute-done | bytes 92192 | tf_op jit(solution)/shard_map/ppermute | solution.py:18
  86.8 6.1 %select_maximum_fusion = f32[5,18,34,258]{3,2,1,0:T(8,128)S(1)} fusion(f32[5,18,1,256]{3,2,1,0:T(1,128)S(1)} %collective-permute-done.10, f32[5,18,1,256]{3,2,1,0:T(1,128)S(1)} %collective-permute-done.11, f32[5,1,32,256]{3,2,1,0:T(8,128)S(1)} %collective-permute-done.8, f32[5,1,32,256]{3,2,1,0:T(8,128)S(1)} %collective-permute-done.9, ...), kind=kLoop, calls=%fused_computation.6 | loop fusion | flops 12631680 | bytes 6291360 | tf_op jit(solution)/shard_map/concatenate | solution.py:19
  92.9 0.8 slice_subtract_fusion
  93.7 1.2 fusion.25
  95.0 0.0 copy-start.4
  95.0 4.5 %add_add_fusion = f32[5,16,32,256]{3,2,1,0:T(8,128)S(1)} fusion(f32[5,18,34,258]{3,2,1,0:T(8,128)S(1)} %select_maximum_fusion, f32[5,1,32,256]{3,2,1,0:T(8,128)S(1)} %collective-permute-done.8, f32[1,16,32,256]{3,2,1,0:T(8,128)S(1)} %get-tuple-element.10, f32[1,16,32,256]{3,2,1,0:T(8,128)S(1)} %get-tuple-element.9, ...), kind=kLoop, calls=%fused_computation.43 | loop fusion | flops 13762560 | bytes 10997760 | tf_op jit(solution)/shard_map/add | solution.py:30
  99.5 0.7 fusion.31
  100.3 0.5 copy.24
  100.8 0.5 copy.23
  101.4 1.5 fusion.8
  102.8 1.8 pad_maximum_fusion.21
  104.6 1.1 copy.22
  105.7 3.3 %pad_maximum_fusion = f32[5,131072]{1,0:T(8,128)} fusion(f32[1,131072]{1,0:T(1,128)S(1)} %bitcast.53, f32[1,131072]{1,0:T(1,128)S(1)} %bitcast.54, f32[3,131072]{1,0:T(4,128)S(1)} %bitcast.48), kind=kLoop, calls=%fused_computation.21 | loop fusion | flops 1310720 | bytes 5242880 | tf_op jit(solution)/shard_map/concatenate | solution.py:65
  109.0 30.3 %copy.18 = f32[5,131072]{0,1:T(8,128)} copy(f32[5,131072]{1,0:T(8,128)} %pad_maximum_fusion) | data formatting | bytes 5242880 | tf_op jit(solution)/shard_map/concatenate | solution.py:65
  139.3 10.7 %gather_fusion = f32[1024,5]{1,0:T(8,128)S(1)} fusion(f32[5,131072]{0,1:T(8,128)} %copy.18, s32[1024]{0:T(1024)S(1)} %broadcast_clamp_fusion), kind=kCustom, calls=%fused_computation | custom fusion | bytes 45056 | tf_op jit(solution)/shard_map/gather | solution.py:87
  150.0 0.2 slice.384
  150.2 0.2 copy.19
  150.4 0.2 copy.20
  150.7 1.6 fusion.22
  152.2 88.3 %psum.7 = f32[32,384]{0,1:T(8,128)S(1)} all-reduce(f32[32,384]{0,1:T(8,128)S(1)} %fusion.22), channel_id=1, replica_groups=mesh['east'=8,'north'=32] {'east','north'}, use_global_device_ids=true, to_apply=%region_2.3 | all-reduce | flops 12288 | bytes 98304 | tf_op jit(solution)/shard_map/psum | solution.py:106
  240.5 0.7 copy.21
  (39 shorter events, 0.2 us)
Async XLA Ops:
  0.6 19.3 %copy-start = (f32[3,16,32,256]{3,2,1,0:T(8,128)S(1)}, f32[3,16,32,256]{3,2,1,0:T(8,128)}, u32[]{:S(2)}) copy-start(f32[3,16,32,256]{3,2,1,0:T(8,128)} %param.11) | copy-start | bytes 4718596
  0.6 18.3 %copy-start.1 = (f32[16,32,256]{2,1,0:T(8,128)S(1)}, f32[16,32,256]{2,1,0:T(8,128)}, u32[]{:S(2)}) copy-start(f32[16,32,256]{2,1,0:T(8,128)} %param.12) | copy-start | bytes 1572868
  2.5 27.6 %collective-permute-start.5 = (f32[4,1,32,256]{3,2,1,0:T(8,128)}, f32[4,1,32,256]{3,2,1,0:T(8,128)}, u32[]{:S(2)}, u32[]{:S(2)}) collective-permute-start(f32[4,1,32,256]{3,2,1,0:T(8,128)} %get-tuple-element.27), channel_id=1, source_target_pairs={{0,32},{32,64},{64,96},{96,128},{128,160},{160,192},{192,224},{1,3... | collective-permute-start | bytes 393224 | tf_op jit(solution)/shard_map/ppermute | solution.py:17
  8.8 21.4 %collective-permute-start.4 = (f32[4,1,32,256]{3,2,1,0:T(8,128)}, f32[4,1,32,256]{3,2,1,0:T(8,128)}, u32[]{:S(2)}, u32[]{:S(2)}) collective-permute-start(f32[4,1,32,256]{3,2,1,0:T(8,128)} %get-tuple-element.28), channel_id=1, source_target_pairs={{32,0},{64,32},{96,64},{128,96},{160,128},{192,160},{224,192},{33,... | collective-permute-start | bytes 393224 | tf_op jit(solution)/shard_map/ppermute | solution.py:18
  12.5 23.2 %collective-permute-start = (f32[5,1,32,256]{3,2,1,0:T(8,128)}, f32[5,1,32,256]{3,2,1,0:T(8,128)S(1)}, u32[]{:S(2)}, u32[]{:S(2)}) collective-permute-start(f32[5,1,32,256]{3,2,1,0:T(8,128)} %get-tuple-element.23), channel_id=1, source_target_pairs={{32,0},{64,32},{96,64},{128,96},{160,128},{192,160},{224,192},{33,... | collective-permute-start | bytes 491528 | tf_op jit(solution)/shard_map/ppermute | solution.py:18
  14.4 7.0 %copy-start.14 = (s32[1,1,1024]{2,1,0:T(1,128)S(1)}, s32[1,1,1024]{2,1,0:T(1,128)}, u32[]{:S(2)}) copy-start(s32[1,1,1024]{2,1,0:T(1,128)} %param.14) | copy-start | bytes 12292
  14.4 7.0 %copy-start.12 = (s32[1,1,1024]{2,1,0:T(1,128)S(1)}, s32[1,1,1024]{2,1,0:T(1,128)}, u32[]{:S(2)}) copy-start(s32[1,1,1024]{2,1,0:T(1,128)} %param.16) | copy-start | bytes 12292
  14.4 21.3 %collective-permute-start.1 = (f32[5,1,32,256]{3,2,1,0:T(8,128)}, f32[5,1,32,256]{3,2,1,0:T(8,128)S(1)}, u32[]{:S(2)}, u32[]{:S(2)}) collective-permute-start(f32[5,1,32,256]{3,2,1,0:T(8,128)} %get-tuple-element.24), channel_id=1, source_target_pairs={{0,32},{32,64},{64,96},{96,128},{128,160},{160,192},{192,224},{1,3... | collective-permute-start | bytes 491528 | tf_op jit(solution)/shard_map/ppermute | solution.py:17
  30.1 5.6 %copy-start.2 = (f32[5,16,32,256]{3,2,1,0:T(8,128)S(1)}, f32[5,16,32,256]{3,2,1,0:T(8,128)}, u32[]{:S(2)}) copy-start(f32[5,16,32,256]{3,2,1,0:T(8,128)} %param.9) | copy-start | bytes 7864324
  31.2 11.4 %collective-permute-start.7 = (f32[4,18,1,256]{3,2,1,0:T(1,128)S(1)}, f32[4,18,1,256]{3,2,1,0:T(1,128)S(1)}, u32[]{:S(2)}, u32[]{:S(2)}) collective-permute-start(f32[4,18,1,256]{3,2,1,0:T(1,128)S(1)} %get-tuple-element.25), channel_id=1, source_target_pairs={{0,1},{1,2},{2,3},{3,4},{4,5},{5,6},{6,7},{7,8},{8,9},{9,10},{10,1... | collective-permute-start | bytes 221192 | tf_op jit(solution)/shard_map/ppermute | solution.py:17
  34.4 8.3 %collective-permute-start.6 = (f32[4,18,1,256]{3,2,1,0:T(1,128)S(1)}, f32[4,18,1,256]{3,2,1,0:T(1,128)S(1)}, u32[]{:S(2)}, u32[]{:S(2)}) collective-permute-start(f32[4,18,1,256]{3,2,1,0:T(1,128)S(1)} %get-tuple-element.26), channel_id=1, source_target_pairs={{1,0},{2,1},{3,2},{4,3},{5,4},{6,5},{7,6},{8,7},{9,8},{10,9},{11,1... | collective-permute-start | bytes 221192 | tf_op jit(solution)/shard_map/ppermute | solution.py:18
  36.3 11.8 %copy-start.3 = (f32[5,16,32,256]{3,2,1,0:T(8,128)}, f32[5,16,32,256]{3,2,1,0:T(8,128)S(1)}, u32[]{:S(2)}) copy-start(f32[5,16,32,256]{3,2,1,0:T(8,128)S(1)} %get-tuple-element.21) | copy-start | bytes 7864324
  36.5 11.7 %collective-permute-start.3 = (f32[5,18,1,256]{3,2,1,0:T(1,128)S(1)}, f32[5,18,1,256]{3,2,1,0:T(1,128)S(1)}, u32[]{:S(2)}, u32[]{:S(2)}) collective-permute-start(f32[5,18,1,256]{3,2,1,0:T(1,128)S(1)} %get-tuple-element.14), channel_id=1, source_target_pairs={{0,1},{1,2},{2,3},{3,4},{4,5},{5,6},{6,7},{7,8},{8,9},{9,10},{10,1... | collective-permute-start | bytes 276488 | tf_op jit(solution)/shard_map/ppermute | solution.py:17
  40.5 7.7 %collective-permute-start.2 = (f32[5,18,1,256]{3,2,1,0:T(1,128)S(1)}, f32[5,18,1,256]{3,2,1,0:T(1,128)S(1)}, u32[]{:S(2)}, u32[]{:S(2)}) collective-permute-start(f32[5,18,1,256]{3,2,1,0:T(1,128)S(1)} %get-tuple-element.15), channel_id=1, source_target_pairs={{1,0},{2,1},{3,2},{4,3},{5,4},{6,5},{7,6},{8,7},{9,8},{10,9},{11,1... | collective-permute-start | bytes 276488 | tf_op jit(solution)/shard_map/ppermute | solution.py:18
  42.6 5.5 %copy-start.10 = (f32[4,18,1,256]{3,2,1,0:T(1,128)}, f32[4,18,1,256]{3,2,1,0:T(1,128)S(1)}, u32[]{:S(2)}) copy-start(f32[4,18,1,256]{3,2,1,0:T(1,128)S(1)} %collective-permute-done.6) | copy-start | bytes 221188
  51.2 3.7 %copy-start.5 = (f32[16,32,256]{2,1,0:T(8,128)S(1)}, f32[16,32,256]{2,1,0:T(8,128)}, u32[]{:S(2)}) copy-start(f32[16,32,256]{2,1,0:T(8,128)} %get-tuple-element.34) | copy-start | bytes 1572868
  51.2 3.7 %copy-start.6 = (f32[16,32,256]{2,1,0:T(8,128)S(1)}, f32[16,32,256]{2,1,0:T(8,128)}, u32[]{:S(2)}) copy-start(f32[16,32,256]{2,1,0:T(8,128)} %get-tuple-element.30) | copy-start | bytes 1572868
  51.2 3.7 %copy-start.7 = (f32[16,32,256]{2,1,0:T(8,128)S(1)}, f32[16,32,256]{2,1,0:T(8,128)}, u32[]{:S(2)}) copy-start(f32[16,32,256]{2,1,0:T(8,128)} %get-tuple-element.31) | copy-start | bytes 1572868
  63.0 6.7 %copy-start.13 = (f32[1,1,1024]{2,1,0:T(1,128)S(1)}, f32[1,1,1024]{2,1,0:T(1,128)}, u32[]{:S(2)}) copy-start(f32[1,1,1024]{2,1,0:T(1,128)} %param.17) | copy-start | bytes 12292
  63.0 7.0 %collective-permute-start.9 = (f32[5,1,32,256]{3,2,1,0:T(8,128)S(1)}, f32[5,1,32,256]{3,2,1,0:T(8,128)S(1)}, u32[]{:S(2)}, u32[]{:S(2)}) collective-permute-start(f32[5,1,32,256]{3,2,1,0:T(8,128)S(1)} %get-tuple-element.19), channel_id=1, source_target_pairs={{0,32},{32,64},{64,96},{96,128},{128,160},{160,192},{192,224},{1,3... | collective-permute-start | bytes 491528 | tf_op jit(solution)/shard_map/ppermute | solution.py:17
  67.7 7.9 %collective-permute-start.8 = (f32[5,1,32,256]{3,2,1,0:T(8,128)S(1)}, f32[5,1,32,256]{3,2,1,0:T(8,128)S(1)}, u32[]{:S(2)}, u32[]{:S(2)}) collective-permute-start(f32[5,1,32,256]{3,2,1,0:T(8,128)S(1)} %get-tuple-element.20), channel_id=1, source_target_pairs={{32,0},{64,32},{96,64},{128,96},{160,128},{192,160},{224,192},{33,... | collective-permute-start | bytes 491528 | tf_op jit(solution)/shard_map/ppermute | solution.py:18
  75.8 7.5 %collective-permute-start.11 = (f32[5,18,1,256]{3,2,1,0:T(1,128)S(1)}, f32[5,18,1,256]{3,2,1,0:T(1,128)S(1)}, u32[]{:S(2)}, u32[]{:S(2)}) collective-permute-start(f32[5,18,1,256]{3,2,1,0:T(1,128)S(1)} %get-tuple-element.12), channel_id=1, source_target_pairs={{0,1},{1,2},{2,3},{3,4},{4,5},{5,6},{6,7},{7,8},{8,9},{9,10},{10,1... | collective-permute-start | bytes 276488 | tf_op jit(solution)/shard_map/ppermute | solution.py:17
  81.5 5.3 %collective-permute-start.10 = (f32[5,18,1,256]{3,2,1,0:T(1,128)S(1)}, f32[5,18,1,256]{3,2,1,0:T(1,128)S(1)}, u32[]{:S(2)}, u32[]{:S(2)}) collective-permute-start(f32[5,18,1,256]{3,2,1,0:T(1,128)S(1)} %get-tuple-element.13), channel_id=1, source_target_pairs={{1,0},{2,1},{3,2},{4,3},{5,4},{6,5},{7,6},{8,7},{9,8},{10,9},{11,1... | collective-permute-start | bytes 276488 | tf_op jit(solution)/shard_map/ppermute | solution.py:18
  95.0 4.6 %copy-start.4 = (f32[5,16,32,256]{3,2,1,0:T(8,128)S(1)}, f32[5,16,32,256]{3,2,1,0:T(8,128)}, u32[]{:S(2)}) copy-start(f32[5,16,32,256]{3,2,1,0:T(8,128)} %param.10) | copy-start | bytes 7864324
  95.0 4.6 %copy-start.9 = (f32[16,32,256]{2,1,0:T(8,128)S(1)}, f32[16,32,256]{2,1,0:T(8,128)}, u32[]{:S(2)}) copy-start(f32[16,32,256]{2,1,0:T(8,128)} %get-tuple-element.2) | copy-start | bytes 1572868
  99.5 1.8 copy-start.8
  109.0 41.6 %copy-start.11 = (f32[8,1024]{1,0:T(8,128)S(1)}, f32[8,1024]{1,0:T(8,128)}, u32[]{:S(2)}) copy-start(f32[8,1024]{1,0:T(8,128)} %fusion.42) | copy-start | bytes 98308
  109.0 41.6 %copy-start.15 = (s32[1,1,1024]{2,1,0:T(1,128)S(1)}, s32[1,1,1024]{2,1,0:T(1,128)}, u32[]{:S(2)}) copy-start(s32[1,1,1024]{2,1,0:T(1,128)} %param.15) | copy-start | bytes 12292
where the time goes:
time: 242 us; the launch traced here: 241 us
  blocking collectives  88.3 us (36%)
  local copies, waits for them, and re-layouts  56.3 us (23%)
  other arithmetic  45.7 us (19%)
  starting transfers between devices  38 us (16%)
  waiting for transfers between devices  9.52 us (4%)
    psum x1, blocking collectives, shards(): summed = lax.psum(partial_grad, ('east', 'north'))  88.3 us
    concatenate x1, local copies, waits for them, and re-layouts, relax(): return jnp.concatenate([velocity, pressure[None], eddy_new[None]], axis=0)  30.3 us
    ppermute x6, starting transfers between devices, extended(): before = lax.ppermute(last, axis, up)  28.4 us
    concatenate x5, other arithmetic, extended(): shard = jnp.concatenate([before, shard, after], axis=dim)  15.8 us
    gather x1, local copies, waits for them, and re-layouts, shards(): values = flat_state[:, cells]  10.7 us
    ppermute x6, starting transfers between devices, extended(): after = lax.ppermute(leading, axis, down)  9.63 us
    ppermute x6, waiting for transfers between devices, extended(): after = lax.ppermute(leading, axis, down)  9.21 us
    gather x1, local copies, waits for them, and re-layouts, shards(): upstream = base_flow[0].reshape(-1)[cells]  6.15 us
  transfers between devices with their start and end apart: 12, of which 3 were waited for; matrix products, arithmetic and copies ran while one was open for 9% of the time, Pallas kernels for 0%

commit v1 on v0

--- a/solution.py
+++ b/solution.py
@@ -103,7 +103,7 @@
     partial_grad = jnp.dot(
         combined, turbine_hot, precision=lax.Precision.HIGHEST, preferred_element_type=jnp.float32
     )
-    summed = lax.psum(partial_grad, ("east", "north"))
+    summed = lax.psum(lax.psum(partial_grad, "north"), "east")
     owned = lax.dynamic_slice_in_dim(summed, lax.axis_index("north") * TURB_DEV, TURB_DEV, 1)
     return (state, owned.reshape(4, SECT, TURB_DEV))
 

time: 242 us -> 342 us (1.41)
  blocking collectives: 88.3 us -> 185 us
    psum x1 -> x2, blocking collectives: 88.3 us -> 185 us  [shards(): summed = lax.psum(lax.psum(partial_grad, 'north'), 'east')]
  transfers between devices with their start and end apart: 12 -> 12, of which waited for: 3 -> 3; matrix products, arithmetic and copies ran while one was open for 9% -> 6% of each run, Pallas kernels for 0% -> 0%
where the time goes in v1:
time: 342 us; the launch traced here: 341 us
  blocking collectives  185 us (54%)
  local copies, waits for them, and re-layouts  56.6 us (17%)
  other arithmetic  47.9 us (14%)
  starting transfers between devices  38 us (11%)
  waiting for transfers between devices  9.51 us (3%)
    psum x2, blocking collectives, shards(): summed = lax.psum(lax.psum(partial_grad, 'north'), 'east')  185 us
    concatenate x1, local copies, waits for them, and re-layouts, relax(): return jnp.concatenate([velocity, pressure[None], eddy_new[None]], axis=0)  30.3 us
    ppermute x6, starting transfers between devices, extended(): before = lax.ppermute(last, axis, up)  28.4 us
    concatenate x5, other arithmetic, extended(): shard = jnp.concatenate([before, shard, after], axis=dim)  15.6 us
    gather x1, local copies, waits for them, and re-layouts, shards(): values = flat_state[:, cells]  10.7 us
    ppermute x6, starting transfers between devices, extended(): after = lax.ppermute(leading, axis, down)  9.63 us
    ppermute x6, waiting for transfers between devices, extended(): after = lax.ppermute(leading, axis, down)  9.21 us
  transfers between devices with their start and end apart: 12, of which 3 were waited for; matrix products, arithmetic and copies ran while one was open for 6% of the time, Pallas kernels for 0%

profile of v1, /device:TPU:1, one launch (start us, length us, event | category | flops | bytes accessed | tf_op | source)
XLA Modules:
  0.0 340.8 jit_solution(2072387821994143403)
XLA Ops:
  0.6 1.9 pad_maximum_fusion.37
  2.5 6.3 %collective-permute-start.5 = (f32[4,1,32,256]{3,2,1,0:T(8,128)}, f32[4,1,32,256]{3,2,1,0:T(8,128)S(1)}, u32[]{:S(2)}, u32[]{:S(2)}) collective-permute-start(f32[4,1,32,256]{3,2,1,0:T(8,128)} %get-tuple-element.27), channel_id=1, source_target_pairs={{0,32},{32,64},{64,96},{96,128},{128,160},{160,192},{192,224},{1,3... | collective-permute-start | bytes 393224 | tf_op jit(solution)/shard_map/ppermute | solution.py:17
  8.8 1.9 collective-permute-start.4
  10.7 1.8 fusion.45
  12.5 1.9 collective-permute-start
  14.4 0.0 copy-start.19
  14.4 0.0 copy-start.17
  14.4 4.5 %collective-permute-start.1 = (f32[5,1,32,256]{3,2,1,0:T(8,128)}, f32[5,1,32,256]{3,2,1,0:T(8,128)S(1)}, u32[]{:S(2)}, u32[]{:S(2)}) collective-permute-start(f32[5,1,32,256]{3,2,1,0:T(8,128)} %get-tuple-element.24), channel_id=1, source_target_pairs={{0,32},{32,64},{64,96},{96,128},{128,160},{160,192},{192,224},{1,3... | collective-permute-start | bytes 491528 | tf_op jit(solution)/shard_map/ppermute | solution.py:17
  19.0 1.1 broadcast_add_fusion
  20.1 1.2 fusion.46
  21.4 0.6 fusion.42
  22.6 0.3 copy.25
  22.9 6.2 %gather_fusion.1 = f32[1024]{0:T(1024)S(1)} fusion(f32[131072]{0:T(1024)S(1)} %bitcast.42, s32[1024]{0:T(1024)S(1)} %broadcast_clamp_fusion), kind=kCustom, calls=%fused_computation.1 | custom fusion | bytes 12288 | tf_op jit(solution)/shard_map/gather | solution.py:89
  29.1 0.0 copy-start.2
  29.1 0.0 collective-permute-done.4
  29.1 1.0 pad_maximum_fusion.44
  30.1 3.1 collective-permute-start.7
  33.3 1.3 collective-permute-start.6
  34.6 0.6 copy-done.10
  35.3 0.0 collective-permute-done
  35.3 1.9 fusion.2
  37.2 0.9 constant_dynamic-update-slice_fusion
  38.1 0.1 fusion.44
  38.2 4.0 %collective-permute-start.3 = (f32[5,18,1,256]{3,2,1,0:T(1,128)S(1)}, f32[5,18,1,256]{3,2,1,0:T(1,128)S(1)}, u32[]{:S(2)}, u32[]{:S(2)}) collective-permute-start(f32[5,18,1,256]{3,2,1,0:T(1,128)S(1)} %get-tuple-element.14), channel_id=1, source_target_pairs={{0,1},{1,2},{2,3},{3,4},{4,5},{5,6},{6,7},{7,8},{8,9},{9,10},{10,1... | collective-permute-start | bytes 276488 | tf_op jit(solution)/shard_map/ppermute | solution.py:17
  42.2 1.3 collective-permute-start.2
  43.5 0.8 slice.359
  44.4 5.4 %select_maximum_fusion.8 = f32[4,18,34,258]{3,2,1,0:T(8,128)S(1)} fusion(f32[4,18,1,256]{3,2,1,0:T(1,128)S(1)} %collective-permute-done.6, f32[4,18,1,256]{3,2,1,0:T(1,128)S(1)} %collective-permute-done.7, f32[4,1,32,256]{3,2,1,0:T(8,128)} %collective-permute-done.4, f32[4,1,32,256]{3,2,1,0:T(8,128)S(1)} %copy-done.13, f32[1,16,32,256]{3,2,1,0:T(8,128)S(1)} %bitcast.45, ...), kind=kLoop, calls=%fused_computation.15 | loop fusion | flops 8842176 | bytes 5033088 | tf_op jit(solution)/shard_map/concatenate | solution.py:19
  49.8 0.0 collective-permute-done.3
  49.8 3.0 select_maximum_fusion.6
  52.9 4.5 %slice_subtract_fusion.1 = (f32[5,16,32,256]{3,2,1,0:T(8,128)S(1)}, f32[5,16,32,256]{3,2,1,0:T(8,128)S(1)}, f32[5,16,32,256]{3,2,1,0:T(8,128)S(1)}) fusion(f32[5,18,34,258]{3,2,1,0:T(8,128)S(1)} %select_maximum_fusion.6, f32[5,18,32,256]{3,2,1,0:T(8,128)S(1)} %constant_dynamic-update-slice_fusion, f32[5,18,1,256]{3,2,1,0:T(1,128)S(1)} %collective-permute-done.3, ...), kind=kLoop, calls=%fused_computation.46 | loop fusion | flops 7208960 | bytes 19189760 | tf_op jit(solution)/shard_map/sub | solution.py:37
  57.5 5.9 %multiply_reduce_fusion = (f32[16,32,256]{2,1,0:T(8,128)}, f32[16,32,256]{2,1,0:T(8,128)}, f32[3,16,32,256]{3,2,1,0:T(8,128)S(1)}) fusion(f32[5,16,32,256]{3,2,1,0:T(8,128)S(1)} %copy-done.2, f32[16,32,256]{2,1,0:T(8,128)} %get-tuple-element.34, f32[1,16,32,256]{3,2,1,0:T(8,128)S(1)} %slice.361, f32[1,16,32,256]{3,2,1,0:T(8,128)S(1)} %slice.360, ...), kind=kLoop, calls=%fused_computation.92 | loop fusion | flops 14286848 | bytes 21905408 | tf_op jit(solution)/shard_map/reduce_sum | solution.py:63
  63.4 1.9 fusion.37
  65.3 0.0 copy-start.18
  65.4 4.7 %collective-permute-start.9 = (f32[5,1,32,256]{3,2,1,0:T(8,128)S(1)}, f32[5,1,32,256]{3,2,1,0:T(8,128)S(1)}, u32[]{:S(2)}, u32[]{:S(2)}) collective-permute-start(f32[5,1,32,256]{3,2,1,0:T(8,128)S(1)} %get-tuple-element.19), channel_id=1, source_target_pairs={{0,32},{32,64},{64,96},{96,128},{128,160},{160,192},{192,224},{1,3... | collective-permute-start | bytes 491528 | tf_op jit(solution)/shard_map/ppermute | solution.py:17
  70.1 1.9 collective-permute-start.8
  72.0 0.3 collective-permute-done.9
  72.3 5.7 %collective-permute-done.8 = f32[5,1,32,256]{3,2,1,0:T(8,128)S(1)} collective-permute-done((f32[5,1,32,256]{3,2,1,0:T(8,128)S(1)}, f32[5,1,32,256]{3,2,1,0:T(8,128)S(1)}, u32[]{:S(2)}, u32[]{:S(2)}) %collective-permute-start.8) | collective-permute-done | bytes 163872 | tf_op jit(solution)/shard_map/ppermute | solution.py:18
  78.0 0.1 pad_maximum_fusion.39
  78.1 5.7 %collective-permute-start.11 = (f32[5,18,1,256]{3,2,1,0:T(1,128)S(1)}, f32[5,18,1,256]{3,2,1,0:T(1,128)S(1)}, u32[]{:S(2)}, u32[]{:S(2)}) collective-permute-start(f32[5,18,1,256]{3,2,1,0:T(1,128)S(1)} %get-tuple-element.12), channel_id=1, source_target_pairs={{0,1},{1,2},{2,3},{3,4},{4,5},{5,6},{6,7},{7,8},{8,9},{9,10},{10,1... | collective-permute-start | bytes 276488 | tf_op jit(solution)/shard_map/ppermute | solution.py:17
  83.9 1.3 collective-permute-start.10
  85.2 0.4 fusion.23
  85.6 3.5 %collective-permute-done.10 = f32[5,18,1,256]{3,2,1,0:T(1,128)S(1)} collective-permute-done((f32[5,18,1,256]{3,2,1,0:T(1,128)S(1)}, f32[5,18,1,256]{3,2,1,0:T(1,128)S(1)}, u32[]{:S(2)}, u32[]{:S(2)}) %collective-permute-start.10) | collective-permute-done | bytes 92192 | tf_op jit(solution)/shard_map/ppermute | solution.py:18
  89.2 6.1 %select_maximum_fusion = f32[5,18,34,258]{3,2,1,0:T(8,128)S(1)} fusion(f32[5,18,1,256]{3,2,1,0:T(1,128)S(1)} %collective-permute-done.10, f32[5,18,1,256]{3,2,1,0:T(1,128)S(1)} %collective-permute-done.11, f32[5,1,32,256]{3,2,1,0:T(8,128)S(1)} %collective-permute-done.8, f32[5,1,32,256]{3,2,1,0:T(8,128)S(1)} %collective-permute-done.9, ...), kind=kLoop, calls=%fused_computation.6 | loop fusion | flops 12631680 | bytes 6291360 | tf_op jit(solution)/shard_map/concatenate | solution.py:19
  95.2 0.8 slice_subtract_fusion
  96.1 1.2 fusion.25
  97.3 0.0 copy-start.3
  97.3 4.5 %add_add_fusion = f32[5,16,32,256]{3,2,1,0:T(8,128)S(1)} fusion(f32[5,18,34,258]{3,2,1,0:T(8,128)S(1)} %select_maximum_fusion, f32[5,1,32,256]{3,2,1,0:T(8,128)S(1)} %collective-permute-done.8, f32[1,16,32,256]{3,2,1,0:T(8,128)S(1)} %get-tuple-element.10, f32[1,16,32,256]{3,2,1,0:T(8,128)S(1)} %get-tuple-element.9, ...), kind=kLoop, calls=%fused_computation.43 | loop fusion | flops 13762560 | bytes 10997760 | tf_op jit(solution)/shard_map/add | solution.py:30
  101.9 0.0 copy-start.4
  102.0 0.7 fusion.31
  102.7 0.5 copy.24
  103.2 0.5 copy.23
  103.8 1.5 fusion.8
  105.3 1.8 pad_maximum_fusion.21
  107.1 1.1 copy.22
  108.2 3.4 pad_maximum_fusion
  111.5 30.3 %copy.18 = f32[5,131072]{0,1:T(8,128)} copy(f32[5,131072]{1,0:T(8,128)} %pad_maximum_fusion) | data formatting | bytes 5242880 | tf_op jit(solution)/shard_map/concatenate | solution.py:65
  141.8 10.7 %gather_fusion = f32[1024,5]{1,0:T(8,128)S(1)} fusion(f32[5,131072]{0,1:T(8,128)} %copy.18, s32[1024]{0:T(1024)S(1)} %broadcast_clamp_fusion), kind=kCustom, calls=%fused_computation | custom fusion | bytes 45056 | tf_op jit(solution)/shard_map/gather | solution.py:87
  152.6 0.2 slice.384
  152.8 0.2 copy.19
  152.9 0.2 copy.20
  153.2 1.6 fusion.22
  154.8 129.1 %psum.14 = f32[32,384]{0,1:T(8,128)S(1)} all-reduce(f32[32,384]{0,1:T(8,128)S(1)} %fusion.22), channel_id=1, replica_groups=mesh['east'=8,'north'=32] {'north'}, use_global_device_ids=true, to_apply=%region_2.3 | all-reduce | flops 12288 | bytes 98304 | tf_op jit(solution)/shard_map/psum | solution.py:106
  283.9 56.2 %psum.15 = f32[32,384]{0,1:T(8,128)S(1)} all-reduce(f32[32,384]{0,1:T(8,128)S(1)} %psum.14), channel_id=1, replica_groups=mesh['east'=8,'north'=32] {'east'}, use_global_device_ids=true, to_apply=%region_3.4 | all-reduce | flops 12288 | bytes 98304 | tf_op jit(solution)/shard_map/psum | solution.py:106
  340.1 0.7 copy.21
  (50 shorter events, 0.3 us)
Async XLA Ops:
  0.6 19.5 %copy-start = (f32[3,16,32,256]{3,2,1,0:T(8,128)S(1)}, f32[3,16,32,256]{3,2,1,0:T(8,128)}, u32[]{:S(2)}) copy-start(f32[3,16,32,256]{3,2,1,0:T(8,128)} %param.11) | copy-start | bytes 4718596
  0.6 18.3 %copy-start.1 = (f32[16,32,256]{2,1,0:T(8,128)S(1)}, f32[16,32,256]{2,1,0:T(8,128)}, u32[]{:S(2)}) copy-start(f32[16,32,256]{2,1,0:T(8,128)} %param.12) | copy-start | bytes 1572868
  2.5 26.6 %collective-permute-start.5 = (f32[4,1,32,256]{3,2,1,0:T(8,128)}, f32[4,1,32,256]{3,2,1,0:T(8,128)S(1)}, u32[]{:S(2)}, u32[]{:S(2)}) collective-permute-start(f32[4,1,32,256]{3,2,1,0:T(8,128)} %get-tuple-element.27), channel_id=1, source_target_pairs={{0,32},{32,64},{64,96},{96,128},{128,160},{160,192},{192,224},{1,3... | collective-permute-start | bytes 393224 | tf_op jit(solution)/shard_map/ppermute | solution.py:17
  8.8 20.3 %collective-permute-start.4 = (f32[4,1,32,256]{3,2,1,0:T(8,128)}, f32[4,1,32,256]{3,2,1,0:T(8,128)}, u32[]{:S(2)}, u32[]{:S(2)}) collective-permute-start(f32[4,1,32,256]{3,2,1,0:T(8,128)} %get-tuple-element.28), channel_id=1, source_target_pairs={{32,0},{64,32},{96,64},{128,96},{160,128},{192,160},{224,192},{33,... | collective-permute-start | bytes 393224 | tf_op jit(solution)/shard_map/ppermute | solution.py:18
  12.5 22.8 %collective-permute-start = (f32[5,1,32,256]{3,2,1,0:T(8,128)}, f32[5,1,32,256]{3,2,1,0:T(8,128)}, u32[]{:S(2)}, u32[]{:S(2)}) collective-permute-start(f32[5,1,32,256]{3,2,1,0:T(8,128)} %get-tuple-element.23), channel_id=1, source_target_pairs={{32,0},{64,32},{96,64},{128,96},{160,128},{192,160},{224,192},{33,... | collective-permute-start | bytes 491528 | tf_op jit(solution)/shard_map/ppermute | solution.py:18
  14.4 6.9 %copy-start.19 = (s32[1,1,1024]{2,1,0:T(1,128)S(1)}, s32[1,1,1024]{2,1,0:T(1,128)}, u32[]{:S(2)}) copy-start(s32[1,1,1024]{2,1,0:T(1,128)} %param.14) | copy-start | bytes 12292
  14.4 6.9 %copy-start.17 = (s32[1,1,1024]{2,1,0:T(1,128)S(1)}, s32[1,1,1024]{2,1,0:T(1,128)}, u32[]{:S(2)}) copy-start(s32[1,1,1024]{2,1,0:T(1,128)} %param.16) | copy-start | bytes 12292
  14.4 20.1 %collective-permute-start.1 = (f32[5,1,32,256]{3,2,1,0:T(8,128)}, f32[5,1,32,256]{3,2,1,0:T(8,128)S(1)}, u32[]{:S(2)}, u32[]{:S(2)}) collective-permute-start(f32[5,1,32,256]{3,2,1,0:T(8,128)} %get-tuple-element.24), channel_id=1, source_target_pairs={{0,32},{32,64},{64,96},{96,128},{128,160},{160,192},{192,224},{1,3... | collective-permute-start | bytes 491528 | tf_op jit(solution)/shard_map/ppermute | solution.py:17
  29.1 6.2 %copy-start.2 = (f32[5,16,32,256]{3,2,1,0:T(8,128)S(1)}, f32[5,16,32,256]{3,2,1,0:T(8,128)}, u32[]{:S(2)}) copy-start(f32[5,16,32,256]{3,2,1,0:T(8,128)} %param.9) | copy-start | bytes 7864324
  29.1 5.5 %copy-start.12 = (f32[4,1,32,256]{3,2,1,0:T(8,128)}, f32[4,1,32,256]{3,2,1,0:T(8,128)S(1)}, u32[]{:S(2)}) copy-start(f32[4,1,32,256]{3,2,1,0:T(8,128)S(1)} %collective-permute-done.5) | copy-start | bytes 393220
  30.1 14.2 %collective-permute-start.7 = (f32[4,18,1,256]{3,2,1,0:T(1,128)S(1)}, f32[4,18,1,256]{3,2,1,0:T(1,128)S(1)}, u32[]{:S(2)}, u32[]{:S(2)}) collective-permute-start(f32[4,18,1,256]{3,2,1,0:T(1,128)S(1)} %get-tuple-element.25), channel_id=1, source_target_pairs={{0,1},{1,2},{2,3},{3,4},{4,5},{5,6},{6,7},{7,8},{8,9},{9,10},{10,1... | collective-permute-start | bytes 221192 | tf_op jit(solution)/shard_map/ppermute | solution.py:17
  33.3 11.1 %collective-permute-start.6 = (f32[4,18,1,256]{3,2,1,0:T(1,128)S(1)}, f32[4,18,1,256]{3,2,1,0:T(1,128)S(1)}, u32[]{:S(2)}, u32[]{:S(2)}) collective-permute-start(f32[4,18,1,256]{3,2,1,0:T(1,128)S(1)} %get-tuple-element.26), channel_id=1, source_target_pairs={{1,0},{2,1},{3,2},{4,3},{5,4},{6,5},{7,6},{8,7},{9,8},{10,9},{11,1... | collective-permute-start | bytes 221192 | tf_op jit(solution)/shard_map/ppermute | solution.py:18
  34.6 0.7 copy-start.10
  35.3 9.1 %copy-start.13 = (f32[4,1,32,256]{3,2,1,0:T(8,128)S(1)}, f32[4,1,32,256]{3,2,1,0:T(8,128)}, u32[]{:S(2)}) copy-start(f32[4,1,32,256]{3,2,1,0:T(8,128)} %copy-done.12) | copy-start | bytes 393220
  38.2 11.6 %collective-permute-start.3 = (f32[5,18,1,256]{3,2,1,0:T(1,128)S(1)}, f32[5,18,1,256]{3,2,1,0:T(1,128)S(1)}, u32[]{:S(2)}, u32[]{:S(2)}) collective-permute-start(f32[5,18,1,256]{3,2,1,0:T(1,128)S(1)} %get-tuple-element.14), channel_id=1, source_target_pairs={{0,1},{1,2},{2,3},{3,4},{4,5},{5,6},{6,7},{7,8},{8,9},{9,10},{10,1... | collective-permute-start | bytes 276488 | tf_op jit(solution)/shard_map/ppermute | solution.py:17
  42.2 7.6 %collective-permute-start.2 = (f32[5,18,1,256]{3,2,1,0:T(1,128)S(1)}, f32[5,18,1,256]{3,2,1,0:T(1,128)S(1)}, u32[]{:S(2)}, u32[]{:S(2)}) collective-permute-start(f32[5,18,1,256]{3,2,1,0:T(1,128)S(1)} %get-tuple-element.15), channel_id=1, source_target_pairs={{1,0},{2,1},{3,2},{4,3},{5,4},{6,5},{7,6},{8,7},{9,8},{10,9},{11,1... | collective-permute-start | bytes 276488 | tf_op jit(solution)/shard_map/ppermute | solution.py:18
  44.4 5.4 %copy-start.14 = (f32[4,18,1,256]{3,2,1,0:T(1,128)}, f32[4,18,1,256]{3,2,1,0:T(1,128)S(1)}, u32[]{:S(2)}) copy-start(f32[4,18,1,256]{3,2,1,0:T(1,128)S(1)} %collective-permute-done.7) | copy-start | bytes 221188
  44.4 5.4 %copy-start.15 = (f32[4,18,1,256]{3,2,1,0:T(1,128)}, f32[4,18,1,256]{3,2,1,0:T(1,128)S(1)}, u32[]{:S(2)}) copy-start(f32[4,18,1,256]{3,2,1,0:T(1,128)S(1)} %collective-permute-done.6) | copy-start | bytes 221188
  49.8 3.1 copy-start.11
  65.3 6.7 %copy-start.18 = (f32[1,1,1024]{2,1,0:T(1,128)S(1)}, f32[1,1,1024]{2,1,0:T(1,128)}, u32[]{:S(2)}) copy-start(f32[1,1,1024]{2,1,0:T(1,128)} %param.17) | copy-start | bytes 12292
  65.4 7.0 %collective-permute-start.9 = (f32[5,1,32,256]{3,2,1,0:T(8,128)S(1)}, f32[5,1,32,256]{3,2,1,0:T(8,128)S(1)}, u32[]{:S(2)}, u32[]{:S(2)}) collective-permute-start(f32[5,1,32,256]{3,2,1,0:T(8,128)S(1)} %get-tuple-element.19), channel_id=1, source_target_pairs={{0,32},{32,64},{64,96},{96,128},{128,160},{160,192},{192,224},{1,3... | collective-permute-start | bytes 491528 | tf_op jit(solution)/shard_map/ppermute | solution.py:17
  70.1 7.9 %collective-permute-start.8 = (f32[5,1,32,256]{3,2,1,0:T(8,128)S(1)}, f32[5,1,32,256]{3,2,1,0:T(8,128)S(1)}, u32[]{:S(2)}, u32[]{:S(2)}) collective-permute-start(f32[5,1,32,256]{3,2,1,0:T(8,128)S(1)} %get-tuple-element.20), channel_id=1, source_target_pairs={{32,0},{64,32},{96,64},{128,96},{160,128},{192,160},{224,192},{33,... | collective-permute-start | bytes 491528 | tf_op jit(solution)/shard_map/ppermute | solution.py:18
  78.1 7.5 %collective-permute-start.11 = (f32[5,18,1,256]{3,2,1,0:T(1,128)S(1)}, f32[5,18,1,256]{3,2,1,0:T(1,128)S(1)}, u32[]{:S(2)}, u32[]{:S(2)}) collective-permute-start(f32[5,18,1,256]{3,2,1,0:T(1,128)S(1)} %get-tuple-element.12), channel_id=1, source_target_pairs={{0,1},{1,2},{2,3},{3,4},{4,5},{5,6},{6,7},{7,8},{8,9},{9,10},{10,1... | collective-permute-start | bytes 276488 | tf_op jit(solution)/shard_map/ppermute | solution.py:17
  83.9 5.3 %collective-permute-start.10 = (f32[5,18,1,256]{3,2,1,0:T(1,128)S(1)}, f32[5,18,1,256]{3,2,1,0:T(1,128)S(1)}, u32[]{:S(2)}, u32[]{:S(2)}) collective-permute-start(f32[5,18,1,256]{3,2,1,0:T(1,128)S(1)} %get-tuple-element.13), channel_id=1, source_target_pairs={{1,0},{2,1},{3,2},{4,3},{5,4},{6,5},{7,6},{8,7},{9,8},{10,9},{11,1... | collective-permute-start | bytes 276488 | tf_op jit(solution)/shard_map/ppermute | solution.py:18
  97.3 4.6 %copy-start.3 = (f32[5,16,32,256]{3,2,1,0:T(8,128)S(1)}, f32[5,16,32,256]{3,2,1,0:T(8,128)}, u32[]{:S(2)}) copy-start(f32[5,16,32,256]{3,2,1,0:T(8,128)} %param.10) | copy-start | bytes 7864324
  97.3 4.6 %copy-start.9 = (f32[16,32,256]{2,1,0:T(8,128)S(1)}, f32[16,32,256]{2,1,0:T(8,128)}, u32[]{:S(2)}) copy-start(f32[16,32,256]{2,1,0:T(8,128)} %get-tuple-element.2) | copy-start | bytes 1572868
  101.9 1.9 copy-start.4
  101.9 1.9 copy-start.5
  101.9 1.9 copy-start.6
  101.9 1.9 copy-start.7
  102.0 1.9 copy-start.8
  111.5 41.6 %copy-start.16 = (f32[8,1024]{1,0:T(8,128)S(1)}, f32[8,1024]{1,0:T(8,128)}, u32[]{:S(2)}) copy-start(f32[8,1024]{1,0:T(8,128)} %fusion.42) | copy-start | bytes 98308
  111.5 41.6 %copy-start.20 = (s32[1,1,1024]{2,1,0:T(1,128)S(1)}, s32[1,1,1024]{2,1,0:T(1,128)}, u32[]{:S(2)}) copy-start(s32[1,1,1024]{2,1,0:T(1,128)} %param.15) | copy-start | bytes 12292
